TPU v7x, 32 devices: a whole 2x2x4 slice. The times are simulated.
32 devices in a mesh: ctx: 8 (over z, y), fsdp: 4 (over x, core).
Axes of the slice: x: 2, y: 2, z: 4, core: 2. Of those that a mesh axis runs over, the one named last changes fastest.
Arguments:
- inputs: bfloat16 [16, 1024, 640], P('fsdp', 'ctx'), may hold values from -6 to 6
- cotangent: bfloat16 [16, 1024, 640], P('fsdp', 'ctx'), may hold values from -6 to 6
- lengths: int32 [16], P('fsdp'), may hold values from 256 to 1024, as said below
- query_weight: bfloat16 [640, 1024], P('fsdp'), may hold values from -0.25 to 0.25
- key_weight: bfloat16 [640, 256], P('fsdp'), may hold values from -0.25 to 0.25
- value_weight: bfloat16 [640, 256], P('fsdp'), may hold values from -0.25 to 0.25
- out_weight: bfloat16 [1024, 640], P('fsdp'), may hold values from -0.1875 to 0.1875
- gate_weight: bfloat16 [640, 2048], P('fsdp'), may hold values from -0.25 to 0.25
- up_weight: bfloat16 [640, 2048], P('fsdp'), may hold values from -0.25 to 0.25
- down_weight: bfloat16 [2048, 640], P('fsdp'), may hold values from -0.125 to 0.125
- pre_attn_gain: bfloat16 [640], P('fsdp'), may hold values from -0.5 to 0.5
- post_attn_gain: bfloat16 [640], P('fsdp'), may hold values from -0.5 to 0.5
- pre_ffw_gain: bfloat16 [640], P('fsdp'), may hold values from -0.5 to 0.5
- post_ffw_gain: bfloat16 [640], P('fsdp'), may hold values from -0.5 to 0.5
- query_gain: bfloat16 [256], P('fsdp'), may hold values from 0 to 0.796875
- key_gain: bfloat16 [256], P('fsdp'), may hold values from 0 to 0.796875
Outputs:
- outputs: bfloat16 [16, 1024, 640], P('fsdp', 'ctx')
- input_grad: bfloat16 [16, 1024, 640], P('fsdp', 'ctx')
- query_weight_grad: float32 [640, 1024], P('fsdp')
- key_weight_grad: float32 [640, 256], P('fsdp')
- value_weight_grad: float32 [640, 256], P('fsdp')
- out_weight_grad: float32 [1024, 640], P('fsdp')
- gate_weight_grad: float32 [640, 2048], P('fsdp')
- up_weight_grad: float32 [640, 2048], P('fsdp')
- down_weight_grad: float32 [2048, 640], P('fsdp')
- pre_attn_gain_grad: float32 [640], P('fsdp')
- post_attn_gain_grad: float32 [640], P('fsdp')
- pre_ffw_gain_grad: float32 [640], P('fsdp')
- post_ffw_gain_grad: float32 [640], P('fsdp')
- query_gain_grad: float32 [256], P('fsdp')
- key_gain_grad: float32 [256], P('fsdp')
Inputs may be any that keep to these rules, and one draw needn't show every extreme that they name: Sequence s has its first lengths[s] positions live; later keys are excluded from every softmax. In each aligned block of 4 sequences exactly one, drawn from the seed, has all 1024 positions live.
All inputs are finite; a program needn't handle non-finite values.
Results may differ from a plain program's by a relative error of at most 0.022.
Values may be sent and summed in bfloat16 or wider, within the bound.
A program may use at most 256 MiB of HBM per device.

v0:
```python
import math
import jax
import jax.numpy as jnp
from jax import lax
from jax.sharding import PartitionSpec as P

EPSILON = 1e-06
MASKED_SCORE = -1e30
ROPE_BASE = 1000000.0


def norm_gain(values, gain_vec):
    return (
        values
        * lax.rsqrt(jnp.mean(values * values, axis=-1, keepdims=True) + EPSILON)
        * (1.0 + gain_vec)
    )


def rotate(values, positions):
    half_dim = values.shape[-1] // 2
    inverse = ROPE_BASE ** (-(jnp.arange(half_dim).astype(jnp.float32) * 2.0) / values.shape[-1])
    angles = positions.astype(jnp.float32)[:, None] * inverse[None, :]
    cosine = jnp.cos(angles)[:, None, :]
    sine_part = jnp.sin(angles)[:, None, :]
    first_half = values[..., :half_dim]
    second_half = values[..., half_dim:]
    return jnp.concatenate(
        [
            first_half * cosine - second_half * sine_part,
            second_half * cosine + first_half * sine_part,
        ],
        axis=-1,
    )


def gelu_mix(gate_in, up_in):
    return jax.nn.gelu(gate_in, approximate=True) * up_in


def body(
    inputs,
    cotangent,
    lengths,
    query_weight,
    key_weight,
    value_weight,
    out_weight,
    gate_weight,
    up_weight,
    down_weight,
    pre_attn_gain,
    post_attn_gain,
    pre_ffw_gain,
    post_ffw_gain,
    query_gain,
    key_gain,
):
    seq_count, row_count, model_width = inputs.shape
    gathered = (
        lax.all_gather(query_weight, "fsdp", axis=0, tiled=True),
        lax.all_gather(key_weight, "fsdp", axis=0, tiled=True),
        lax.all_gather(value_weight, "fsdp", axis=0, tiled=True),
        lax.all_gather(out_weight, "fsdp", axis=0, tiled=True),
        lax.all_gather(gate_weight, "fsdp", axis=0, tiled=True),
        lax.all_gather(up_weight, "fsdp", axis=0, tiled=True),
        lax.all_gather(down_weight, "fsdp", axis=0, tiled=True),
        lax.all_gather(pre_attn_gain, "fsdp", axis=0, tiled=True),
        lax.all_gather(post_attn_gain, "fsdp", axis=0, tiled=True),
        lax.all_gather(pre_ffw_gain, "fsdp", axis=0, tiled=True),
        lax.all_gather(post_ffw_gain, "fsdp", axis=0, tiled=True),
        lax.all_gather(query_gain, "fsdp", axis=0, tiled=True),
        lax.all_gather(key_gain, "fsdp", axis=0, tiled=True),
    )
    (
        query_full,
        key_full,
        value_full,
        out_full,
        gate_full,
        up_full,
        down_full,
        gain_attn_in,
        gain_attn_out,
        gain_ffw_in,
        gain_ffw_out,
        gain_query,
        gain_key,
    ) = gathered
    gain_attn_in = gain_attn_in.astype(jnp.float32)
    gain_attn_out = gain_attn_out.astype(jnp.float32)
    gain_ffw_in = gain_ffw_in.astype(jnp.float32)
    gain_ffw_out = gain_ffw_out.astype(jnp.float32)
    gain_query = gain_query.astype(jnp.float32)
    gain_key = gain_key.astype(jnp.float32)
    head_dim = key_full.shape[1]
    head_count = query_full.shape[1] // head_dim
    seq_len = row_count * lax.axis_size("ctx")
    key_span = math.gcd(512, seq_len)
    att_scale = head_dim ** (-0.5)
    flat_rows = seq_count * row_count
    positions = lax.axis_index("ctx") * row_count + jnp.arange(row_count, dtype=jnp.int32)
    x_flat = inputs.astype(jnp.float32).reshape(flat_rows, model_width)
    attn_in, attn_in_back = jax.vjp(norm_gain, x_flat, gain_attn_in)
    attn_in_b = attn_in.astype(jnp.bfloat16)
    query_lin = jnp.dot(attn_in_b, query_full, preferred_element_type=jnp.float32)
    key_lin = jnp.dot(attn_in_b, key_full, preferred_element_type=jnp.float32)
    value_lin = jnp.dot(attn_in_b, value_full, preferred_element_type=jnp.float32)

    def query_side(lin_values, gain_vec):
        return rotate(
            norm_gain(lin_values.reshape(seq_count, row_count, head_count, head_dim), gain_vec),
            positions,
        )

    def key_side(lin_values, gain_vec):
        return rotate(
            norm_gain(lin_values.reshape(seq_count, row_count, 1, head_dim), gain_vec), positions
        )[:, :, 0, :]

    query_rot, query_side_back = jax.vjp(query_side, query_lin, gain_query)
    key_rot, key_side_back = jax.vjp(key_side, key_lin, gain_key)
    query_b = query_rot.astype(jnp.bfloat16)
    key_b = key_rot.astype(jnp.bfloat16)
    value_b = value_lin.reshape(seq_count, row_count, head_dim).astype(jnp.bfloat16)

    def allowed(key_begin, key_count):
        key_pos = key_begin + jnp.arange(key_count, dtype=jnp.int32)
        causal = key_pos[None, :] <= positions[:, None]
        live = key_pos[None, :] < lengths[:, None]
        return (causal[None] & live[:, None, :])[:, None]

    def raw_scores(key_piece):
        return (
            jnp.einsum("sqhd,skd->shqk", query_b, key_piece, preferred_element_type=jnp.float32)
            * att_scale
        )

    stat_shape = (seq_count, head_count, row_count)
    running_max = jnp.full(stat_shape, MASKED_SCORE, jnp.float32)
    key_piece = lax.all_gather(key_b, "ctx", axis=1, tiled=True)
    value_piece = lax.all_gather(value_b, "ctx", axis=1, tiled=True)
    mask_now = allowed(jnp.int32(0), key_piece.shape[1])
    scores = jnp.where(mask_now, raw_scores(key_piece), MASKED_SCORE)
    new_max = jnp.maximum(running_max, jnp.max(scores, axis=-1))
    weights = jnp.where(mask_now, jnp.exp(scores - new_max[..., None]), 0.0)
    new_sum = jnp.sum(weights, axis=-1)
    new_acc = jnp.einsum(
        "shqk,skd->shqd",
        weights.astype(jnp.bfloat16),
        value_piece,
        preferred_element_type=jnp.float32,
    )
    final_state = (new_max, new_sum, new_acc)
    final_max, final_sum, final_acc = final_state
    attended = final_acc / final_sum[..., None]
    log_total = final_max + jnp.log(final_sum)
    attended_b = (
        attended.transpose(0, 2, 1, 3)
        .reshape(flat_rows, head_count * head_dim)
        .astype(jnp.bfloat16)
    )
    attn_lin = jnp.dot(attended_b, out_full, preferred_element_type=jnp.float32)
    attn_post, attn_post_back = jax.vjp(norm_gain, attn_lin, gain_attn_out)
    middle = x_flat + attn_post
    ffw_in, ffw_in_back = jax.vjp(norm_gain, middle, gain_ffw_in)
    ffw_in_b = ffw_in.astype(jnp.bfloat16)
    gate_lin = jnp.dot(ffw_in_b, gate_full, preferred_element_type=jnp.float32)
    up_lin = jnp.dot(ffw_in_b, up_full, preferred_element_type=jnp.float32)
    hidden, hidden_back = jax.vjp(gelu_mix, gate_lin, up_lin)
    hidden_b = hidden.astype(jnp.bfloat16)
    ffw_out = jnp.dot(hidden_b, down_full, preferred_element_type=jnp.float32)
    ffw_post, ffw_post_back = jax.vjp(norm_gain, ffw_out, gain_ffw_out)
    outputs = (middle + ffw_post).astype(jnp.bfloat16).reshape(seq_count, row_count, model_width)
    grad_top = cotangent.astype(jnp.float32).reshape(flat_rows, model_width)
    d_ffw_out, grad_ffw_out_gain = ffw_post_back(grad_top)
    d_ffw_out_b = d_ffw_out.astype(jnp.bfloat16)
    grad_down = jnp.einsum("rf,rd->fd", hidden_b, d_ffw_out_b, preferred_element_type=jnp.float32)
    d_hidden = jnp.einsum("rd,fd->rf", d_ffw_out_b, down_full, preferred_element_type=jnp.float32)
    d_gate, d_up = hidden_back(d_hidden)
    d_gate_b = d_gate.astype(jnp.bfloat16)
    d_up_b = d_up.astype(jnp.bfloat16)
    grad_gate = jnp.einsum("rd,rf->df", ffw_in_b, d_gate_b, preferred_element_type=jnp.float32)
    grad_up = jnp.einsum("rd,rf->df", ffw_in_b, d_up_b, preferred_element_type=jnp.float32)
    d_ffw_in = jnp.einsum(
        "rf,df->rd", d_gate_b, gate_full, preferred_element_type=jnp.float32
    ) + jnp.einsum("rf,df->rd", d_up_b, up_full, preferred_element_type=jnp.float32)
    d_middle_part, grad_ffw_in_gain = ffw_in_back(d_ffw_in)
    d_middle = grad_top + d_middle_part
    d_attn_lin, grad_attn_out_gain = attn_post_back(d_middle)
    d_attn_b = d_attn_lin.astype(jnp.bfloat16)
    grad_projection = jnp.einsum(
        "ro,rd->od", attended_b, d_attn_b, preferred_element_type=jnp.float32
    )
    d_attended_b = (
        jnp.einsum("rd,od->ro", d_attn_b, out_full, preferred_element_type=jnp.float32)
        .astype(jnp.bfloat16)
        .reshape(seq_count, row_count, head_count, head_dim)
    )
    d_attended = d_attended_b.astype(jnp.float32)
    row_delta = jnp.einsum("sqhd,shqd->shq", d_attended, attended, precision=lax.Precision.HIGHEST)

    def key_grads(key_piece, value_piece, key_begin):
        mask_now = allowed(key_begin, key_piece.shape[1])
        probabilities = jnp.where(
            mask_now, jnp.exp(raw_scores(key_piece) - log_total[..., None]), 0.0
        )
        d_probs = jnp.einsum(
            "sqhd,skd->shqk", d_attended_b, value_piece, preferred_element_type=jnp.float32
        )
        d_scores = (probabilities * (d_probs - row_delta[..., None])).astype(jnp.bfloat16)
        d_query = (
            jnp.einsum("shqk,skd->sqhd", d_scores, key_piece, preferred_element_type=jnp.float32)
            * att_scale
        )
        d_key = (
            jnp.einsum("shqk,sqhd->skd", d_scores, query_b, preferred_element_type=jnp.float32)
            * att_scale
        )
        d_value = jnp.einsum(
            "shqk,sqhd->skd",
            probabilities.astype(jnp.bfloat16),
            d_attended_b,
            preferred_element_type=jnp.float32,
        )
        return (d_query, jnp.concatenate([d_key, d_value], axis=-1))

    key_back_all, value_back_all = (
        lax.all_gather(key_b, "ctx", axis=1, tiled=True),
        lax.all_gather(value_b, "ctx", axis=1, tiled=True),
    )

    def slice_keys(key_begin, key_count):
        return (
            lax.dynamic_slice_in_dim(key_back_all, key_begin, key_count, 1),
            lax.dynamic_slice_in_dim(value_back_all, key_begin, key_count, 1),
        )

    query_zero = jnp.zeros((seq_count, row_count, head_count, head_dim), jnp.float32)

    def joint_step(block_id, state):
        d_query_sum, key_buffer = state
        key_begin = block_id * key_span
        key_piece, value_piece = slice_keys(key_begin, key_span)
        d_query, d_keyval = key_grads(key_piece, value_piece, key_begin)
        return (
            d_query_sum + d_query,
            lax.dynamic_update_slice_in_dim(key_buffer, d_keyval, key_begin, 1),
        )

    d_query_rot, key_buffer = lax.fori_loop(
        0,
        seq_len // key_span,
        joint_step,
        (query_zero, jnp.zeros((seq_count, seq_len, 2 * head_dim), jnp.float32)),
    )
    d_keyval_own = lax.psum_scatter(key_buffer, "ctx", scatter_dimension=1, tiled=True)
    d_key_rot = d_keyval_own[..., :head_dim]
    d_value = d_keyval_own[..., head_dim:]
    d_query_lin, grad_query_gain = query_side_back(d_query_rot)
    d_key_lin, grad_key_gain = key_side_back(d_key_rot)
    d_query_b = d_query_lin.astype(jnp.bfloat16)
    d_key_b = d_key_lin.astype(jnp.bfloat16)
    d_value_b = d_value.reshape(flat_rows, head_dim).astype(jnp.bfloat16)
    grad_query = jnp.einsum("rd,rq->dq", attn_in_b, d_query_b, preferred_element_type=jnp.float32)
    grad_key = jnp.einsum("rd,rq->dq", attn_in_b, d_key_b, preferred_element_type=jnp.float32)
    grad_value = jnp.einsum("rd,rq->dq", attn_in_b, d_value_b, preferred_element_type=jnp.float32)
    d_attn_in = jnp.einsum("rq,dq->rd", d_query_b, query_full, preferred_element_type=jnp.float32)
    d_attn_in = d_attn_in + jnp.einsum(
        "rq,dq->rd", d_key_b, key_full, preferred_element_type=jnp.float32
    )
    d_attn_in = d_attn_in + jnp.einsum(
        "rq,dq->rd", d_value_b, value_full, preferred_element_type=jnp.float32
    )
    d_input_part, grad_attn_in_gain = attn_in_back(d_attn_in)
    input_grad = (
        (d_middle + d_input_part).astype(jnp.bfloat16).reshape(seq_count, row_count, model_width)
    )
    shards = (
        lax.psum_scatter(
            grad_query.astype(jnp.bfloat16), "fsdp", scatter_dimension=0, tiled=True
        ).astype(jnp.float32),
        lax.psum_scatter(
            grad_key.astype(jnp.bfloat16), "fsdp", scatter_dimension=0, tiled=True
        ).astype(jnp.float32),
        lax.psum_scatter(
            grad_value.astype(jnp.bfloat16), "fsdp", scatter_dimension=0, tiled=True
        ).astype(jnp.float32),
        lax.psum_scatter(
            grad_projection.astype(jnp.bfloat16), "fsdp", scatter_dimension=0, tiled=True
        ).astype(jnp.float32),
        lax.psum_scatter(
            grad_gate.astype(jnp.bfloat16), "fsdp", scatter_dimension=0, tiled=True
        ).astype(jnp.float32),
        lax.psum_scatter(
            grad_up.astype(jnp.bfloat16), "fsdp", scatter_dimension=0, tiled=True
        ).astype(jnp.float32),
        lax.psum_scatter(
            grad_down.astype(jnp.bfloat16), "fsdp", scatter_dimension=0, tiled=True
        ).astype(jnp.float32),
        lax.psum_scatter(
            grad_attn_in_gain.astype(jnp.bfloat16), "fsdp", scatter_dimension=0, tiled=True
        ).astype(jnp.float32),
        lax.psum_scatter(
            grad_attn_out_gain.astype(jnp.bfloat16), "fsdp", scatter_dimension=0, tiled=True
        ).astype(jnp.float32),
        lax.psum_scatter(
            grad_ffw_in_gain.astype(jnp.bfloat16), "fsdp", scatter_dimension=0, tiled=True
        ).astype(jnp.float32),
        lax.psum_scatter(
            grad_ffw_out_gain.astype(jnp.bfloat16), "fsdp", scatter_dimension=0, tiled=True
        ).astype(jnp.float32),
        lax.psum_scatter(
            grad_query_gain.astype(jnp.bfloat16), "fsdp", scatter_dimension=0, tiled=True
        ).astype(jnp.float32),
        lax.psum_scatter(
            grad_key_gain.astype(jnp.bfloat16), "fsdp", scatter_dimension=0, tiled=True
        ).astype(jnp.float32),
    )
    totals = lax.psum(
        (
            shards[0],
            shards[1],
            shards[2],
            shards[3],
            shards[4],
            shards[5],
            shards[6],
            shards[7],
            shards[8],
            shards[9],
            shards[10],
            shards[11],
            shards[12],
        ),
        "ctx",
    )
    return (outputs, input_grad) + tuple(totals)


def solution(mesh):
    in_specs = (
        P("fsdp", "ctx", None),
        P("fsdp", "ctx", None),
        P("fsdp"),
        P("fsdp", None),
        P("fsdp", None),
        P("fsdp", None),
        P("fsdp", None),
        P("fsdp", None),
        P("fsdp", None),
        P("fsdp", None),
        P("fsdp"),
        P("fsdp"),
        P("fsdp"),
        P("fsdp"),
        P("fsdp"),
        P("fsdp"),
    )
    out_specs = (
        P("fsdp", "ctx", None),
        P("fsdp", "ctx", None),
        P("fsdp", None),
        P("fsdp", None),
        P("fsdp", None),
        P("fsdp", None),
        P("fsdp", None),
        P("fsdp", None),
        P("fsdp", None),
        P("fsdp"),
        P("fsdp"),
        P("fsdp"),
        P("fsdp"),
        P("fsdp"),
        P("fsdp"),
    )
    return jax.shard_map(body, mesh=mesh, in_specs=in_specs, out_specs=out_specs, check_vma=False)
```

profile of v0, /device:TPU:0, one launch (start us, length us, event | category | flops | bytes accessed | tf_op | source)
XLA Modules:
  0.0 893.9 jit_solution(16385621297810421104)
XLA Ops:
  17.0 9.2 %all-reduce.18 = (bf16[256]{0:T(256)(128)(2,1)S(1)}, bf16[640]{0:T(1024)(128)(2,1)S(1)}, bf16[256]{0:T(256)(128)(2,1)S(1)}, bf16[640]{0:T(1024)(128)(2,1)S(1)}, ...) all-reduce(bf16[256]{0:T(256)(128)(2,1)S(1)} %dynamic-update-slice., ...), channel_id=1, replica_groups=mesh['ctx'=8,'fsdp'=4] {'fsdp'}, use_global_device_ids=true, to_apply=%add.5 | all-reduce | flops 3072 | bytes 12288
  26.3 6.2 all_gather.48
  36.3 6.2 all_gather.53
  58.8 27.3 %all-gather.21.cloned.1.call-done = bf16[4,1024,1,256]{3,1,0,2:T(8,128)(2,1)} async-done(((bf16[4,128,1,256]{3,1,0,2:T(8,128)(2,1)}), bf16[4,1024,1,256]{3,1,0,2:T(8,128)(2,1)}) %all-gather.21.cloned.1.call-update) | async-done | bytes 2097168 | tf_op jit(solution)/shard_map/all_gather | solution.py:141
  94.9 41.7 %all-gather.11.cloned.1.call-done = bf16[4,1024,256]{2,1,0:T(8,128)(2,1)} async-done(((bf16[4,128,256]{2,1,0:T(8,128)(2,1)}), bf16[4,1024,256]{2,1,0:T(8,128)(2,1)}) %all-gather.11.cloned.1.call-update) | async-done | bytes 2097168 | tf_op jit(solution)/shard_map/all_gather | solution.py:142
  136.6 8.1 fusion.45
  146.8 8.0 all-gather.13.cloned.1.call-done
  160.6 21.1 %all-gather.15.cloned.1.call-done = bf16[640,2048]{1,0:T(8,128)(2,1)} async-done(((bf16[160,2048]{1,0:T(8,128)(2,1)}), bf16[640,2048]{1,0:T(8,128)(2,1)}) %all-gather.15.cloned.1.call-update) | async-done | bytes 2621456 | tf_op jit(solution)/shard_map/all_gather | solution.py:65
  181.7 5.8 fusion.78
  187.5 21.2 %all-gather.17.cloned.1.call-done = bf16[640,2048]{1,0:T(8,128)(2,1)} async-done(((bf16[160,2048]{1,0:T(8,128)(2,1)}), bf16[640,2048]{1,0:T(8,128)(2,1)}) %all-gather.17.cloned.1.call-update) | async-done | bytes 2621456 | tf_op jit(solution)/shard_map/all_gather | solution.py:66
  208.7 8.3 multiply_convert_fusion.1
  217.0 18.9 %all-gather.19.cloned.1.call-done = bf16[2048,640]{1,0:T(8,128)(2,1)} async-done(((bf16[512,640]{1,0:T(8,128)(2,1)}), bf16[2048,640]{1,0:T(8,128)(2,1)}) %all-gather.19.cloned.1.call-update) | async-done | bytes 2621456 | tf_op jit(solution)/shard_map/all_gather | solution.py:67
  277.6 40.3 %while.16 = (s32[]{:T(128)}, f32[4,128,4,256]{1,3,2,0:T(8,128)S(1)}, f32[4,1024,512]{2,1,0:T(8,128)}, bf16[4,1024,256]{2,1,0:T(8,128)(2,1)}, s32[4]{0:T(128)S(1)...) while((s32[]{:T(128)}, ...), condition=%wide.region_12.13_spmd.clone, body=%wide.region_11.12_spmd.clone.sunk | while | flops 2698316288 | bytes 81694016 | solution.py:251
  288.1 5.3 copy.128
  308.0 5.3 copy.128
  338.3 4.9 convolution_convert_fusion
  348.7 5.6 reduce-scatter.11.cloned.1.call-done
  354.4 37.1 %reduce-scatter.19.cloned.1.call-done = bf16[160,2048]{1,0:T(8,128)(2,1)} async-done(((bf16[640,2048]{1,0:T(8,128)(2,1)}), bf16[160,2048]{1,0:T(8,128)(2,1)}) %reduce-scatter.19.cloned.1.call-update) | async-done | bytes 655376 | tf_op jit(solution)/shard_map/reduce_scatter | solution.py:292
  391.5 37.4 %reduce-scatter.21.cloned.1.call-done = bf16[160,2048]{1,0:T(8,128)(2,1)} async-done(((bf16[640,2048]{1,0:T(8,128)(2,1)}), bf16[160,2048]{1,0:T(8,128)(2,1)}) %reduce-scatter.21.cloned.1.call-update) | async-done | bytes 655376 | tf_op jit(solution)/shard_map/reduce_scatter | solution.py:295
  428.9 37.1 %reduce-scatter.23.cloned.1.call-done = bf16[512,640]{1,0:T(8,128)(2,1)} async-done(((bf16[2048,640]{1,0:T(8,128)(2,1)}), bf16[512,640]{1,0:T(8,128)(2,1)}) %reduce-scatter.23.cloned.1.call-update) | async-done | bytes 655376 | tf_op jit(solution)/shard_map/reduce_scatter | solution.py:298
  466.0 153.5 %reduce-scatter.9.cloned.1.call-done = f32[4,128,512]{2,1,0:T(8,128)} async-done(((f32[4,1024,512]{2,1,0:T(8,128)}), f32[4,128,512]{2,1,0:T(8,128)}) %reduce-scatter.9.cloned.1.call-update) | async-done | bytes 1048592 | tf_op jit(solution)/shard_map/reduce_scatter | solution.py:257
  627.2 7.1 all-reduce.17
  641.9 23.6 %reduce-scatter.13.cloned.1.call-done = bf16[160,256]{1,0:T(8,128)(2,1)} async-done(((bf16[640,256]{1,0:T(8,128)(2,1)}), bf16[160,256]{1,0:T(8,128)(2,1)}) %reduce-scatter.13.cloned.1.call-update) | async-done | bytes 81936 | tf_op jit(solution)/shard_map/reduce_scatter | solution.py:283
  665.5 221.7 %all-reduce.20 = (f32[160,1024]{1,0:T(8,128)}, f32[160,256]{1,0:T(8,128)}, f32[160,256]{1,0:T(8,128)}, f32[256,640]{1,0:T(8,128)}, f32[160,2048]{1,0:T(8,128)}, ...) all-reduce(bf16[160,1024]{1,0:T(8,128)(2,1)} %reduce-scatter.11.clo, ...), channel_id=1, replica_groups=mesh['ctx'=8,'fsdp'=4] {'ctx'}, use_global_device_ids=true, to_apply=%region_18.19 | all-reduce | flops 1393408 | bytes 8361984 | tf_op jit(solution)/shard_map/psum | solution.py:320
  (302 shorter events, 155.0 us)
Async XLA Ops:
  7.2 41.3 %all-gather.9.cloned.1.call-start = ((), (), s32[]{:S(2)}) async-start(), calls=%async_computation.8 | async-start | bytes 1638400 | tf_op jit(solution)/shard_map/all_gather | solution.py:61
  7.9 78.1 %all-gather.21.cloned.1.call-start = ((), (), s32[]{:S(2)}) async-start(), calls=%async_computation.22 | async-start | bytes 2359296 | tf_op jit(solution)/shard_map/all_gather | solution.py:141
  11.9 30.6 %copy-start.51 = (f32[4,128]{1,0:T(4,128)}, f32[4,128]{1,0:T(4,128)S(1)}, u32[]{:S(2)}) copy-start(f32[4,128]{1,0:T(4,128)S(1)} %fusion.58) | copy-start | bytes 6148
  11.9 20.5 %copy-start.47 = (f32[512]{0:T(512)}, f32[512]{0:T(512)S(1)}, u32[]{:S(2)}) copy-start(f32[512]{0:T(512)S(1)} %bitcast_rsqrt_fusion.1) | copy-start | bytes 6148
  34.7 19.6 %copy-start.25 = (f32[128,128]{1,0:T(8,128)}, f32[128,128]{1,0:T(8,128)S(1)}, u32[]{:S(2)}) copy-start(f32[128,128]{1,0:T(8,128)S(1)} %get-tuple-element.348) | copy-start | bytes 196612
  34.7 19.6 %copy-start.27 = (f32[128,128]{1,0:T(8,128)}, f32[128,128]{1,0:T(8,128)S(1)}, u32[]{:S(2)}) copy-start(f32[128,128]{1,0:T(8,128)S(1)} %get-tuple-element.349) | copy-start | bytes 196612
  36.2 100.4 %all-gather.11.cloned.1.call-start = ((), (), s32[]{:S(2)}) async-start(), calls=%async_computation.9 | async-start | bytes 2359296 | tf_op jit(solution)/shard_map/all_gather | solution.py:142
  43.9 110.9 %all-gather.13.cloned.1.call-start = ((), (), s32[]{:S(2)}) async-start(), calls=%async_computation.10 | async-start | bytes 1638400 | tf_op jit(solution)/shard_map/all_gather | solution.py:64
  44.4 137.3 %all-gather.15.cloned.1.call-start = ((), (), s32[]{:S(2)}) async-start(), calls=%async_computation.11 | async-start | bytes 3276800 | tf_op jit(solution)/shard_map/all_gather | solution.py:65
  45.0 163.7 %all-gather.17.cloned.1.call-start = ((), (), s32[]{:S(2)}) async-start(), calls=%async_computation.12 | async-start | bytes 3276800 | tf_op jit(solution)/shard_map/all_gather | solution.py:66
  45.6 190.3 %all-gather.19.cloned.1.call-start = ((), (), s32[]{:S(2)}) async-start(), calls=%async_computation.13 | async-start | bytes 3276800 | tf_op jit(solution)/shard_map/all_gather | solution.py:67
  46.4 302.3 %reduce-scatter.17.cloned.1.call-start = ((), (), s32[]{:S(2)}) async-start(), calls=%async_computation.18 | async-start | bytes 1638400 | tf_op jit(solution)/shard_map/reduce_scatter | solution.py:289
  270.2 84.1 %reduce-scatter.11.cloned.1.call-start = ((), (), s32[]{:S(2)}) async-start(), calls=%async_computation.15 | async-start | bytes 1638400 | tf_op jit(solution)/shard_map/reduce_scatter | solution.py:280
  327.6 63.9 %reduce-scatter.19.cloned.1.call-start = ((), (), s32[]{:S(2)}) async-start(), calls=%async_computation.19 | async-start | bytes 3276800 | tf_op jit(solution)/shard_map/reduce_scatter | solution.py:292
  332.3 96.6 %reduce-scatter.21.cloned.1.call-start = ((), (), s32[]{:S(2)}) async-start(), calls=%async_computation.20 | async-start | bytes 3276800 | tf_op jit(solution)/shard_map/reduce_scatter | solution.py:295
  337.3 128.8 %reduce-scatter.23.cloned.1.call-start = ((), (), s32[]{:S(2)}) async-start(), calls=%async_computation.21 | async-start | bytes 3276800 | tf_op jit(solution)/shard_map/reduce_scatter | solution.py:298
  343.3 276.2 %reduce-scatter.9.cloned.1.call-start = ((), (), s32[]{:S(2)}) async-start(), calls=%async_computation.14 | async-start | bytes 9437184 | tf_op jit(solution)/shard_map/reduce_scatter | solution.py:257
  344.0 297.9 %reduce-scatter.15.cloned.1.call-start = ((), (), s32[]{:S(2)}) async-start(), calls=%async_computation.17 | async-start | bytes 409600 | tf_op jit(solution)/shard_map/reduce_scatter | solution.py:286
  348.7 273.4 %copy-start.9 = (f32[512,256]{1,0:T(8,128)S(1)}, f32[512,256]{1,0:T(8,128)}, u32[]{:S(2)}) copy-start(f32[512,256]{1,0:T(8,128)} %copy-done.8) | copy-start | bytes 1572868
  348.7 273.4 %copy-start.50 = (f32[4,128]{1,0:T(4,128)S(1)}, f32[4,128]{1,0:T(4,128)}, u32[]{:S(2)}) copy-start(f32[4,128]{1,0:T(4,128)} %copy-done.49) | copy-start | bytes 6148
  348.7 273.4 %copy-start.57 = (f32[256]{0:T(256)S(1)}, f32[256]{0:T(256)}, u32[]{:S(2)}) copy-start(f32[256]{0:T(256)} %copy-done.56) | copy-start | bytes 3076
  622.0 43.4 %reduce-scatter.13.cloned.1.call-start = ((), (), s32[]{:S(2)}) async-start(), calls=%async_computation.16 | async-start | bytes 409600 | tf_op jit(solution)/shard_map/reduce_scatter | solution.py:283
  635.7 29.7 %copy-start.36 = (bf16[160,2048]{1,0:T(8,128)(2,1)S(1)}, bf16[160,2048]{1,0:T(8,128)(2,1)}, u32[]{:S(2)}) copy-start(bf16[160,2048]{1,0:T(8,128)(2,1)} %reduce-scatter.19.cloned.1.call-done) | copy-start | bytes 1966084
  635.7 29.7 %copy-start.37 = (bf16[160,2048]{1,0:T(8,128)(2,1)S(1)}, bf16[160,2048]{1,0:T(8,128)(2,1)}, u32[]{:S(2)}) copy-start(bf16[160,2048]{1,0:T(8,128)(2,1)} %reduce-scatter.21.cloned.1.call-done) | copy-start | bytes 1966084
  (62 other events, 193.3 us)
Sparse Core Ops, SparseCore 0:
  9.6 21.7 all-gather.8
  36.3 49.7 all-gather.20
  88.8 47.7 all-gather.10
  138.0 16.6 all-gather.12
  156.1 25.5 all-gather.14
  183.1 25.5 all-gather.16
  210.3 25.5 all-gather.18
  270.3 26.5 reduce-scatter.16
  327.7 26.6 reduce-scatter.10
  356.7 34.6 reduce-scatter.18
  394.2 34.6 reduce-scatter.20
  431.3 34.6 reduce-scatter.22
  470.1 149.3 reduce-scatter.8
  622.4 19.4 reduce-scatter.14
  645.0 20.4 reduce-scatter.12
where the time goes:
time: 902 us; the launch traced here: 894 us
  waiting for transfers between devices  440 us (49%)
  blocking collectives  250 us (28%)
  matrix products  88.8 us (10%)
  local copies, waits for them, and re-layouts  62.2 us (7%)
  other arithmetic  33.9 us (4%)
  between operations  17.6 us (2%)
    psum x1, blocking collectives, body(): lax.psum((shards[0], shards[1], shards[2], shards[3], shards[4], shards[5...  222 us
    reduce_scatter x1, waiting for transfers between devices, body(): lax.psum_scatter(key_buffer, 'ctx', scatter_dimension=1, tiled=True)  153 us
    all_gather x1, waiting for transfers between devices, body(): value_piece = lax.all_gather(value_b, 'ctx', axis=1, tiled=True)  41.7 us
    reduce_scatter x1, waiting for transfers between devices, body(): lax.psum_scatter(grad_up.astype(jnp.bfloat16), 'fsdp', scatter_dimension=...  37.4 us
    reduce_scatter x1, waiting for transfers between devices, body(): lax.psum_scatter(grad_down.astype(jnp.bfloat16), 'fsdp', scatter_dimensio...  37.1 us
    reduce_scatter x1, waiting for transfers between devices, body(): lax.psum_scatter(grad_gate.astype(jnp.bfloat16), 'fsdp', scatter_dimensio...  37.1 us
    all_gather x1, waiting for transfers between devices, body(): key_piece = lax.all_gather(key_b, 'ctx', axis=1, tiled=True)  27.3 us
    unnamed x147, local copies, waits for them, and re-layouts  25.9 us
  transfers between devices with their start and end apart: 15, of which 13 were waited for; matrix products, arithmetic and copies ran while one was open for 15% of the time, Pallas kernels for 0%

commit v1 on v0

--- a/solution.py
+++ b/solution.py
@@ -138,8 +138,11 @@
 
     stat_shape = (seq_count, head_count, row_count)
     running_max = jnp.full(stat_shape, MASKED_SCORE, jnp.float32)
-    key_piece = lax.all_gather(key_b, "ctx", axis=1, tiled=True)
-    value_piece = lax.all_gather(value_b, "ctx", axis=1, tiled=True)
+    key_piece, value_piece = jnp.split(
+        lax.all_gather(jnp.concatenate([key_b, value_b], axis=0), "ctx", axis=1, tiled=True),
+        [key_b.shape[0]],
+        axis=0,
+    )
     mask_now = allowed(jnp.int32(0), key_piece.shape[1])
     scores = jnp.where(mask_now, raw_scores(key_piece), MASKED_SCORE)
     new_max = jnp.maximum(running_max, jnp.max(scores, axis=-1))

time: 902 us -> 947 us (1.050)
  waiting for transfers between devices: 440 us -> 490 us
    all_gather x2 -> x3, waiting for transfers between devices: 69 us -> 122 us  [the longest x1 57.5 us: body(): lax.all_gather(jnp.concatenate([key_b, value_b], axis=0), 'ctx', axis=1,...]
    unnamed x147 -> x149, local copies, waits for them, and re-layouts: 25.9 us -> 22.4 us
  transfers between devices with their start and end apart: 15 -> 16, of which waited for: 13 -> 14; matrix products, arithmetic and copies ran while one was open for 15% -> 17% of each run, Pallas kernels for 0% -> 0%
where the time goes in v1:
time: 947 us; the launch traced here: 937 us
  waiting for transfers between devices  490 us (52%)
  blocking collectives  250 us (26%)
  matrix products  84.7 us (9%)
  local copies, waits for them, and re-layouts  58.8 us (6%)
  other arithmetic  34.5 us (4%)
  between operations  17.7 us (2%)
    psum x1, blocking collectives, body(): lax.psum((shards[0], shards[1], shards[2], shards[3], shards[4], shards[5...  222 us
    reduce_scatter x1, waiting for transfers between devices, body(): lax.psum_scatter(key_buffer, 'ctx', scatter_dimension=1, tiled=True)  153 us
    all_gather x1, waiting for transfers between devices, body(): lax.all_gather(jnp.concatenate([key_b, value_b], axis=0), 'ctx', axis=1,...  57.5 us
    all_gather x1, waiting for transfers between devices, body(): lax.all_gather(key_b, 'ctx', axis=1, tiled=True)  50 us
    reduce_scatter x1, waiting for transfers between devices, body(): lax.psum_scatter(grad_gate.astype(jnp.bfloat16), 'fsdp', scatter_dimensio...  37.3 us
    reduce_scatter x1, waiting for transfers between devices, body(): lax.psum_scatter(grad_up.astype(jnp.bfloat16), 'fsdp', scatter_dimension=...  37.3 us
    reduce_scatter x1, waiting for transfers between devices, body(): lax.psum_scatter(grad_down.astype(jnp.bfloat16), 'fsdp', scatter_dimensio...  37.2 us
    reduce_scatter x1, waiting for transfers between devices, body(): lax.psum_scatter(grad_key.astype(jnp.bfloat16), 'fsdp', scatter_dimension...  23.6 us
  transfers between devices with their start and end apart: 16, of which 14 were waited for; matrix products, arithmetic and copies ran while one was open for 17% of the time, Pallas kernels for 0%

profile of v1, /device:TPU:0, one launch (start us, length us, event | category | flops | bytes accessed | tf_op | source)
XLA Modules:
  0.0 937.4 jit_solution(4269235646652778134)
XLA Ops:
  17.0 9.2 all-reduce.18
  26.2 6.2 all_gather.49
  35.8 6.2 all_gather.51
  60.1 57.5 %all-gather.10.cloned.1.call-done = bf16[8,1024,256]{2,1,0:T(8,128)(2,1)} async-done(((bf16[8,128,256]{2,1,0:T(8,128)(2,1)}), bf16[8,1024,256]{2,1,0:T(8,128)(2,1)}) %all-gather.10.cloned.1.call-update) | async-done | bytes 4194320 | tf_op jit(solution)/shard_map/all_gather | solution.py:142
  129.5 6.2 all-gather.14.cloned.1.call-done
  141.5 21.1 %all-gather.16.cloned.1.call-done = bf16[640,2048]{1,0:T(8,128)(2,1)} async-done(((bf16[160,2048]{1,0:T(8,128)(2,1)}), bf16[640,2048]{1,0:T(8,128)(2,1)}) %all-gather.16.cloned.1.call-update) | async-done | bytes 2621456 | tf_op jit(solution)/shard_map/all_gather | solution.py:65
  162.6 5.8 fusion.77
  168.4 21.2 %all-gather.18.cloned.1.call-done = bf16[640,2048]{1,0:T(8,128)(2,1)} async-done(((bf16[160,2048]{1,0:T(8,128)(2,1)}), bf16[640,2048]{1,0:T(8,128)(2,1)}) %all-gather.18.cloned.1.call-update) | async-done | bytes 2621456 | tf_op jit(solution)/shard_map/all_gather | solution.py:66
  189.6 8.3 multiply_convert_fusion.1
  197.9 18.7 %all-gather.20.cloned.1.call-done = bf16[2048,640]{1,0:T(8,128)(2,1)} async-done(((bf16[512,640]{1,0:T(8,128)(2,1)}), bf16[2048,640]{1,0:T(8,128)(2,1)}) %all-gather.20.cloned.1.call-update) | async-done | bytes 2621456 | tf_op jit(solution)/shard_map/all_gather | solution.py:67
  254.1 14.1 %all-gather.22.cloned.1.call-done = bf16[4,1024,256]{2,1,0:T(8,128)(2,1)} async-done(((bf16[4,128,256]{2,1,0:T(8,128)(2,1)}), bf16[4,1024,256]{2,1,0:T(8,128)(2,1)}) %all-gather.22.cloned.1.call-update) | async-done | bytes 2097168 | tf_op jit(solution)/shard_map/all_gather | solution.py:233
  268.1 50.0 %all-gather.24.cloned.1.call-done = bf16[4,1024,1,256]{3,1,0,2:T(8,128)(2,1)} async-done(((bf16[4,128,1,256]{3,1,0,2:T(8,128)(2,1)}), bf16[4,1024,1,256]{3,1,0,2:T(8,128)(2,1)}) %all-gather.24.cloned.1.call-update) | async-done | bytes 2097168 | tf_op jit(solution)/shard_map/all_gather | solution.py:232
  322.5 40.5 %while.16 = (s32[]{:T(128)}, f32[4,128,4,256]{1,3,2,0:T(8,128)S(1)}, f32[4,1024,512]{2,1,0:T(8,128)}, bf16[4,1024,256]{2,1,0:T(8,128)(2,1)}, s32[4]{0:T(128)S(1)...) while((s32[]{:T(128)}, ...), condition=%wide.region_12.13_spmd.clone, body=%wide.region_11.12_spmd.clone.sunk | while | flops 2698316288 | bytes 81694016 | solution.py:254
  333.1 5.3 copy.128
  353.1 5.3 copy.128
  377.5 4.9 convolution_convert_fusion.1
  383.5 4.9 convolution_convert_fusion
  397.8 37.3 %reduce-scatter.19.cloned.1.call-done = bf16[160,2048]{1,0:T(8,128)(2,1)} async-done(((bf16[640,2048]{1,0:T(8,128)(2,1)}), bf16[160,2048]{1,0:T(8,128)(2,1)}) %reduce-scatter.19.cloned.1.call-update) | async-done | bytes 655376 | tf_op jit(solution)/shard_map/reduce_scatter | solution.py:295
  435.1 37.3 %reduce-scatter.21.cloned.1.call-done = bf16[160,2048]{1,0:T(8,128)(2,1)} async-done(((bf16[640,2048]{1,0:T(8,128)(2,1)}), bf16[160,2048]{1,0:T(8,128)(2,1)}) %reduce-scatter.21.cloned.1.call-update) | async-done | bytes 655376 | tf_op jit(solution)/shard_map/reduce_scatter | solution.py:298
  472.4 37.2 %reduce-scatter.23.cloned.1.call-done = bf16[512,640]{1,0:T(8,128)(2,1)} async-done(((bf16[2048,640]{1,0:T(8,128)(2,1)}), bf16[512,640]{1,0:T(8,128)(2,1)}) %reduce-scatter.23.cloned.1.call-update) | async-done | bytes 655376 | tf_op jit(solution)/shard_map/reduce_scatter | solution.py:301
  509.6 153.3 %reduce-scatter.9.cloned.1.call-done = f32[4,128,512]{2,1,0:T(8,128)} async-done(((f32[4,1024,512]{2,1,0:T(8,128)}), f32[4,128,512]{2,1,0:T(8,128)}) %reduce-scatter.9.cloned.1.call-update) | async-done | bytes 1048592 | tf_op jit(solution)/shard_map/reduce_scatter | solution.py:260
  670.7 7.1 all-reduce.17
  685.3 23.6 %reduce-scatter.13.cloned.1.call-done = bf16[160,256]{1,0:T(8,128)(2,1)} async-done(((bf16[640,256]{1,0:T(8,128)(2,1)}), bf16[160,256]{1,0:T(8,128)(2,1)}) %reduce-scatter.13.cloned.1.call-update) | async-done | bytes 81936 | tf_op jit(solution)/shard_map/reduce_scatter | solution.py:286
  708.9 221.7 %all-reduce.20 = (f32[160,1024]{1,0:T(8,128)}, f32[160,256]{1,0:T(8,128)}, f32[160,256]{1,0:T(8,128)}, f32[256,640]{1,0:T(8,128)}, f32[160,2048]{1,0:T(8,128)}, ...) all-reduce(bf16[160,1024]{1,0:T(8,128)(2,1)} %reduce-scatter.11.clo, ...), channel_id=1, replica_groups=mesh['ctx'=8,'fsdp'=4] {'ctx'}, use_global_device_ids=true, to_apply=%region_18.19 | all-reduce | flops 1393408 | bytes 8361984 | tf_op jit(solution)/shard_map/psum | solution.py:323
  (308 shorter events, 156.6 us)
Async XLA Ops:
  7.2 42.6 %all-gather.12.cloned.1.call-start = ((), (), s32[]{:S(2)}) async-start(), calls=%async_computation.9 | async-start | bytes 1638400 | tf_op jit(solution)/shard_map/all_gather | solution.py:61
  7.9 109.7 %all-gather.10.cloned.1.call-start = ((), (), s32[]{:S(2)}) async-start(), calls=%async_computation.8 | async-start | bytes 4718592 | tf_op jit(solution)/shard_map/all_gather | solution.py:142
  11.9 30.1 %copy-start.50 = (f32[4,128]{1,0:T(4,128)}, f32[4,128]{1,0:T(4,128)S(1)}, u32[]{:S(2)}) copy-start(f32[4,128]{1,0:T(4,128)S(1)} %fusion.56) | copy-start | bytes 6148
  34.7 20.8 %copy-start.25 = (f32[128,128]{1,0:T(8,128)}, f32[128,128]{1,0:T(8,128)S(1)}, u32[]{:S(2)}) copy-start(f32[128,128]{1,0:T(8,128)S(1)} %get-tuple-element.350) | copy-start | bytes 196612
  34.7 20.8 %copy-start.27 = (f32[128,128]{1,0:T(8,128)}, f32[128,128]{1,0:T(8,128)S(1)}, u32[]{:S(2)}) copy-start(f32[128,128]{1,0:T(8,128)S(1)} %get-tuple-element.351) | copy-start | bytes 196612
  43.6 92.0 %all-gather.14.cloned.1.call-start = ((), (), s32[]{:S(2)}) async-start(), calls=%async_computation.10 | async-start | bytes 1638400 | tf_op jit(solution)/shard_map/all_gather | solution.py:64
  44.3 118.3 %all-gather.16.cloned.1.call-start = ((), (), s32[]{:S(2)}) async-start(), calls=%async_computation.11 | async-start | bytes 3276800 | tf_op jit(solution)/shard_map/all_gather | solution.py:65
  44.9 144.7 %all-gather.18.cloned.1.call-start = ((), (), s32[]{:S(2)}) async-start(), calls=%async_computation.12 | async-start | bytes 3276800 | tf_op jit(solution)/shard_map/all_gather | solution.py:66
  45.5 171.1 %all-gather.20.cloned.1.call-start = ((), (), s32[]{:S(2)}) async-start(), calls=%async_computation.13 | async-start | bytes 3276800 | tf_op jit(solution)/shard_map/all_gather | solution.py:67
  46.1 222.1 %all-gather.22.cloned.1.call-start = ((), (), s32[]{:S(2)}) async-start(), calls=%async_computation.14 | async-start | bytes 2359296 | tf_op jit(solution)/shard_map/all_gather | solution.py:233
  46.8 271.3 %all-gather.24.cloned.1.call-start = ((), (), s32[]{:S(2)}) async-start(), calls=%async_computation.23 | async-start | bytes 2359296 | tf_op jit(solution)/shard_map/all_gather | solution.py:232
  47.6 346.1 %reduce-scatter.17.cloned.1.call-start = ((), (), s32[]{:S(2)}) async-start(), calls=%async_computation.19 | async-start | bytes 1638400 | tf_op jit(solution)/shard_map/reduce_scatter | solution.py:292
  251.0 146.8 %reduce-scatter.11.cloned.1.call-start = ((), (), s32[]{:S(2)}) async-start(), calls=%async_computation.16 | async-start | bytes 1638400 | tf_op jit(solution)/shard_map/reduce_scatter | solution.py:283
  372.6 62.5 %reduce-scatter.19.cloned.1.call-start = ((), (), s32[]{:S(2)}) async-start(), calls=%async_computation.20 | async-start | bytes 3276800 | tf_op jit(solution)/shard_map/reduce_scatter | solution.py:295
  377.3 95.1 %reduce-scatter.21.cloned.1.call-start = ((), (), s32[]{:S(2)}) async-start(), calls=%async_computation.21 | async-start | bytes 3276800 | tf_op jit(solution)/shard_map/reduce_scatter | solution.py:298
  382.4 127.2 %reduce-scatter.23.cloned.1.call-start = ((), (), s32[]{:S(2)}) async-start(), calls=%async_computation.22 | async-start | bytes 3276800 | tf_op jit(solution)/shard_map/reduce_scatter | solution.py:301
  388.4 274.5 %reduce-scatter.9.cloned.1.call-start = ((), (), s32[]{:S(2)}) async-start(), calls=%async_computation.15 | async-start | bytes 9437184 | tf_op jit(solution)/shard_map/reduce_scatter | solution.py:260
  389.0 296.3 %reduce-scatter.15.cloned.1.call-start = ((), (), s32[]{:S(2)}) async-start(), calls=%async_computation.18 | async-start | bytes 409600 | tf_op jit(solution)/shard_map/reduce_scatter | solution.py:289
  393.7 271.8 %copy-start.9 = (f32[512,256]{1,0:T(8,128)S(1)}, f32[512,256]{1,0:T(8,128)}, u32[]{:S(2)}) copy-start(f32[512,256]{1,0:T(8,128)} %copy-done.8) | copy-start | bytes 1572868
  393.7 271.9 %copy-start.49 = (f32[4,128]{1,0:T(4,128)S(1)}, f32[4,128]{1,0:T(4,128)}, u32[]{:S(2)}) copy-start(f32[4,128]{1,0:T(4,128)} %copy-done.48) | copy-start | bytes 6148
  393.7 271.9 %copy-start.56 = (f32[256]{0:T(256)S(1)}, f32[256]{0:T(256)}, u32[]{:S(2)}) copy-start(f32[256]{0:T(256)} %copy-done.55) | copy-start | bytes 3076
  665.5 43.4 %reduce-scatter.13.cloned.1.call-start = ((), (), s32[]{:S(2)}) async-start(), calls=%async_computation.17 | async-start | bytes 409600 | tf_op jit(solution)/shard_map/reduce_scatter | solution.py:286
  679.2 29.7 %copy-start.35 = (bf16[160,2048]{1,0:T(8,128)(2,1)S(1)}, bf16[160,2048]{1,0:T(8,128)(2,1)}, u32[]{:S(2)}) copy-start(bf16[160,2048]{1,0:T(8,128)(2,1)} %reduce-scatter.19.cloned.1.call-done) | copy-start | bytes 1966084
  679.2 29.7 %copy-start.36 = (bf16[160,2048]{1,0:T(8,128)(2,1)S(1)}, bf16[160,2048]{1,0:T(8,128)(2,1)}, u32[]{:S(2)}) copy-start(bf16[160,2048]{1,0:T(8,128)(2,1)} %reduce-scatter.21.cloned.1.call-done) | copy-start | bytes 1966084
  (64 other events, 223.0 us)
Sparse Core Ops, SparseCore 0:
  9.6 21.7 all-gather.11
  43.7 73.8 all-gather.9
  119.1 16.4 all-gather.13
  137.0 25.5 all-gather.15
  164.0 25.5 all-gather.17
  191.1 25.5 all-gather.19
  218.8 49.2 all-gather.21
  270.3 47.7 all-gather.23
  320.7 25.0 reduce-scatter.16
  372.7 25.0 reduce-scatter.10
  400.4 34.6 reduce-scatter.18
  437.7 34.6 reduce-scatter.20
  474.9 34.6 reduce-scatter.22
  513.5 149.3 reduce-scatter.8
  665.9 19.4 reduce-scatter.14
  688.4 20.4 reduce-scatter.12
